TPU v7x, 512 devices: a whole 4x8x8 slice. The times are simulated.
512 devices in a mesh: context: 64 (over y_hi, z, core), tensor: 8 (over x, y_lo).
Axes of the slice: x: 4, y: 8 (y_hi: 4, y_lo: 2; y = y_hi * 2 + y_lo), z: 8, core: 2. Of those that a mesh axis runs over, the one named last changes fastest.
Arguments:
- in_gate: bfloat16 [16384, 2048], P('context', 'tensor'), may hold values from -6 to 6
- out_gate: bfloat16 [16384, 2048], P('context', 'tensor'), may hold values from -6 to 6
- values: bfloat16 [16384, 2048], P('context', 'tensor'), may hold values from -6 to 6
- long_filters: float32 [16384, 128], P('context', 'tensor'), may hold values from -1 to 1
- skip_gain: float32 [2048], P('tensor'), may hold values from 0.5 to 2
- projection: bfloat16 [2048, 2048], P('tensor'), may hold values from -0.1875 to 0.1875
Outputs:
- mixed_out: bfloat16 [16384, 2048], P('context', 'tensor')
All inputs are finite; a program needn't handle non-finite values.
Results may differ from a plain program's by a relative error of at most 0.017.
Values may be sent and summed in bfloat16 or wider, within the bound.
No kernel may reach another device: no remote copies, remote signals or barrier semaphores. Data moves between devices by JAX's collectives and lax.ppermute only.
A program may use at most 64 MiB of HBM per device.

v0:
```python
import math

import jax
import jax.numpy as jnp
from jax import lax
from jax.sharding import PartitionSpec as P

HIGHEST = lax.Precision.HIGHEST
TWO_PI = 2.0 * math.pi


def angles(first, second, length):
    product = first[:, None] * second[None, :] % length
    theta = product.astype(jnp.float32) * (TWO_PI / length)
    return (jnp.cos(theta), jnp.sin(theta))


def block_spectrum(signal, blocks):
    count = signal.shape[0]
    cosine, sine = angles(
        jnp.arange(blocks, dtype=jnp.int32), jnp.arange(count, dtype=jnp.int32), blocks
    )
    real = jnp.einsum("qp,pmk->qmk", cosine, signal, precision=HIGHEST)
    imag = -jnp.einsum("qp,pmk->qmk", sine, signal, precision=HIGHEST)
    return (real, imag)


def rotate(real, imag, rows_idx, cols_idx, length, sign):
    cosine, sine = angles(rows_idx, cols_idx, length)
    cosine = cosine[:, :, None]
    sine = sign * sine[:, :, None]
    return (real * cosine - imag * sine, imag * cosine + real * sine)


def inner_transform(real, imag, sign):
    size = real.shape[1]
    index = jnp.arange(size, dtype=jnp.int32)
    cosine, sine = angles(index, index, size)
    sine = sign * sine
    out_real = jnp.einsum("rm,emk->erk", cosine, real, precision=HIGHEST) - jnp.einsum(
        "rm,emk->erk", sine, imag, precision=HIGHEST
    )
    out_imag = jnp.einsum("rm,emk->erk", cosine, imag, precision=HIGHEST) + jnp.einsum(
        "rm,emk->erk", sine, real, precision=HIGHEST
    )
    return (out_real, out_imag)


def block_signal(real, imag, count, length):
    blocks = real.shape[0]
    cosine, sine = angles(
        jnp.arange(count, dtype=jnp.int32), jnp.arange(blocks, dtype=jnp.int32), blocks
    )
    total = jnp.einsum("pq,qmk->pmk", cosine, real, precision=HIGHEST) - jnp.einsum(
        "pq,qmk->pmk", sine, imag, precision=HIGHEST
    )
    return total * (1.0 / length)


def apply_filter(real, imag, width, repeat):
    sig_real = real[..., :width]
    sig_imag = imag[..., :width]
    ker_real = jnp.repeat(real[..., width:], repeat, axis=-1)
    ker_imag = jnp.repeat(imag[..., width:], repeat, axis=-1)
    return (sig_real * ker_real - sig_imag * ker_imag, sig_real * ker_imag + sig_imag * ker_real)


def on_device(in_gate, out_gate, values, long_filters, skip_gain, projection):
    rows, width = in_gate.shape
    contexts = lax.axis_size("context")
    here = lax.axis_index("context")
    blocks = 2 * contexts
    length = blocks * rows
    block_ids = jnp.arange(blocks, dtype=jnp.int32)
    mixed = in_gate.astype(jnp.float32) * values.astype(jnp.float32)
    filt = long_filters.shape[1]
    part = rows // contexts
    signal = jnp.concatenate([mixed, long_filters], axis=1)[None]
    columns = lax.all_to_all(signal, "context", split_axis=1, concat_axis=0, tiled=True)
    real, imag = block_spectrum(columns, blocks)
    offsets = here * part + jnp.arange(part, dtype=jnp.int32)
    real, imag = rotate(real, imag, block_ids, offsets, length, -1.0)
    real, imag = (
        lax.all_to_all(real, "context", split_axis=0, concat_axis=1, tiled=True),
        lax.all_to_all(imag, "context", split_axis=0, concat_axis=1, tiled=True),
    )
    real, imag = inner_transform(real, imag, -1.0)
    real, imag = apply_filter(real, imag, width, width // filt)
    real, imag = inner_transform(real, imag, 1.0)
    real, imag = (
        lax.all_to_all(real, "context", split_axis=1, concat_axis=0, tiled=True),
        lax.all_to_all(imag, "context", split_axis=1, concat_axis=0, tiled=True),
    )
    real, imag = rotate(real, imag, block_ids, offsets, length, 1.0)
    pieces = block_signal(real, imag, contexts, length)
    conv = lax.all_to_all(pieces, "context", split_axis=0, concat_axis=1, tiled=True)[0]
    combined = conv + skip_gain[None, :] * mixed
    gated = (combined * out_gate.astype(jnp.float32)).astype(jnp.bfloat16)
    partial_value = jnp.dot(gated, projection, preferred_element_type=jnp.float32)
    return lax.psum_scatter(
        partial_value.astype(jnp.bfloat16), "tensor", scatter_dimension=1, tiled=True
    )


def solution(mesh):
    return jax.shard_map(
        on_device,
        mesh=mesh,
        in_specs=(
            P("context", "tensor"),
            P("context", "tensor"),
            P("context", "tensor"),
            P("context", "tensor"),
            P("tensor"),
            P("tensor", None),
        ),
        out_specs=P("context", "tensor"),
        check_vma=False,
    )
```

profile of v0, /device:TPU:1, one launch (start us, length us, event | category | flops | bytes accessed | tf_op | source)
XLA Modules:
  0.0 240.1 jit_solution(3849085104319656695)
XLA Ops:
  6.5 0.9 copy.46
  7.4 1.0 convert_multiply_fusion
  8.5 1.2 copy.47
  9.6 17.6 %all-to-all-start = ((f32[1,256,272]{2,0,1:T(1,128)}), f32[1,256,272]{2,0,1:T(1,128)S(1)}, u32[]{:S(2)}, u32[]{:S(2)}) async-start(f32[1,256,272]{2,0,1:T(1,128)} %copy.47), calls=%async_computation | async-start | bytes 786432 | tf_op jit(solution)/shard_map/all_to_all | solution.py:79
  27.4 15.9 %all-to-all-done = f32[1,256,272]{2,0,1:T(1,128)S(1)} async-done(((f32[1,256,272]{2,0,1:T(1,128)}), f32[1,256,272]{2,0,1:T(1,128)S(1)}, u32[]{:S(2)}, u32[]{:S(2)}) %all-to-all-start) | async-done | bytes 278560 | tf_op jit(solution)/shard_map/all_to_all | solution.py:79
  43.3 0.9 reduce
  44.4 1.2 fusion.13
  45.6 1.2 multiply_subtract_fusion
  46.8 1.2 copy.50
  48.0 7.4 %all-to-all-start.1 = ((f32[128,4,272]{2,1,0:T(4,128)}), f32[128,4,272]{2,1,0:T(4,128)S(1)}, u32[]{:S(2)}, u32[]{:S(2)}) async-start(f32[128,4,272]{2,1,0:T(4,128)} %copy.50), calls=%async_computation.1 | async-start | bytes 1572864 | tf_op jit(solution)/shard_map/all_to_all | solution.py:84
  55.4 1.2 copy.53
  56.5 24.4 %all-to-all-done.1 = f32[128,4,272]{2,1,0:T(4,128)S(1)} async-done(((f32[128,4,272]{2,1,0:T(4,128)}), f32[128,4,272]{2,1,0:T(4,128)S(1)}, u32[]{:S(2)}, u32[]{:S(2)}) %all-to-all-start.1) | async-done | bytes 557088 | tf_op jit(solution)/shard_map/all_to_all | solution.py:84
  80.9 6.0 %all-to-all-start.2 = ((f32[128,4,272]{2,1,0:T(4,128)}), f32[128,4,272]{2,1,0:T(4,128)S(1)}, u32[]{:S(2)}, u32[]{:S(2)}) async-start(f32[128,4,272]{2,1,0:T(4,128)} %copy.53), calls=%async_computation.2 | async-start | bytes 1572864 | tf_op jit(solution)/shard_map/all_to_all | solution.py:85
  87.8 1.6 fusion.28
  89.3 21.8 %all-to-all-done.2 = f32[128,4,272]{2,1,0:T(4,128)S(1)} async-done(((f32[128,4,272]{2,1,0:T(4,128)}), f32[128,4,272]{2,1,0:T(4,128)S(1)}, u32[]{:S(2)}, u32[]{:S(2)}) %all-to-all-start.2) | async-done | bytes 557088 | tf_op jit(solution)/shard_map/all_to_all | solution.py:85
  112.0 1.6 fusion.26
  113.6 1.6 fusion.1
  115.2 1.6 fusion
  117.0 1.6 fusion.24
  118.5 1.6 fusion.3
  120.1 1.0 copy.58
  121.1 8.5 %all-to-all-start.3 = ((f32[2,256,256]{2,0,1:T(2,128)}), f32[2,256,256]{2,0,1:T(2,128)S(1)}, u32[]{:S(2)}, u32[]{:S(2)}) async-start(f32[2,256,256]{2,0,1:T(2,128)} %copy.58), calls=%async_computation.3 | async-start | bytes 1048576 | tf_op jit(solution)/shard_map/all_to_all | solution.py:91
  129.7 1.6 fusion.22
  131.2 1.6 fusion.2
  132.8 1.0 copy.61
  133.8 14.9 %all-to-all-done.3 = f32[2,256,256]{2,0,1:T(2,128)S(1)} async-done(((f32[2,256,256]{2,0,1:T(2,128)}), f32[2,256,256]{2,0,1:T(2,128)S(1)}, u32[]{:S(2)}, u32[]{:S(2)}) %all-to-all-start.3) | async-done | bytes 524320 | tf_op jit(solution)/shard_map/all_to_all | solution.py:91
  148.7 6.4 %all-to-all-start.4 = ((f32[2,256,256]{2,0,1:T(2,128)}), f32[2,256,256]{2,0,1:T(2,128)S(1)}, u32[]{:S(2)}, u32[]{:S(2)}) async-start(f32[2,256,256]{2,0,1:T(2,128)} %copy.61), calls=%async_computation.4 | async-start | bytes 1048576 | tf_op jit(solution)/shard_map/all_to_all | solution.py:92
  155.5 18.8 %all-to-all-done.4 = f32[2,256,256]{2,0,1:T(2,128)S(1)} async-done(((f32[2,256,256]{2,0,1:T(2,128)}), f32[2,256,256]{2,0,1:T(2,128)S(1)}, u32[]{:S(2)}, u32[]{:S(2)}) %all-to-all-start.4) | async-done | bytes 524320 | tf_op jit(solution)/shard_map/all_to_all | solution.py:92
  175.4 0.6 fusion.4
  176.2 20.0 %all_to_all.93 = f32[64,4,256]{2,1,0:T(4,128)S(1)} all-to-all(f32[64,4,256]{2,1,0:T(4,128)S(1)} %copy.66), channel_id=1, replica_groups=mesh['context'=64,'tensor'=8] {'context'}, dimensions={0} | all-to-all | bytes 524288 | tf_op jit(solution)/shard_map/all_to_all | solution.py:96
  196.3 1.4 convolution_convert_fusion
  197.8 35.5 %reduce-scatter.2.cloned.1.call-done = bf16[256,256]{1,0:T(8,128)(2,1)} async-done(((bf16[256,2048]{1,0:T(8,128)(2,1)}), bf16[256,256]{1,0:T(8,128)(2,1)}) %reduce-scatter.2.cloned.1.call-update) | async-done | bytes 131088 | tf_op jit(solution)/shard_map/reduce_scatter | solution.py:100
  (35 shorter events, 3.9 us)
Async XLA Ops:
  6.5 189.7 %copy-start = (bf16[256,2048]{1,0:T(8,128)(2,1)S(1)}, bf16[256,2048]{1,0:T(8,128)(2,1)}, u32[]{:S(2)}) copy-start(bf16[256,2048]{1,0:T(8,128)(2,1)} %param.11) | copy-start | bytes 3145732
  9.6 33.7 %all-to-all-start = ((f32[1,256,272]{2,0,1:T(1,128)}), f32[1,256,272]{2,0,1:T(1,128)S(1)}, u32[]{:S(2)}, u32[]{:S(2)}) async-start(f32[1,256,272]{2,0,1:T(1,128)} %copy.47), calls=%async_computation | async-start | bytes 786432 | tf_op jit(solution)/shard_map/all_to_all | solution.py:79
  48.0 32.9 %all-to-all-start.1 = ((f32[128,4,272]{2,1,0:T(4,128)}), f32[128,4,272]{2,1,0:T(4,128)S(1)}, u32[]{:S(2)}, u32[]{:S(2)}) async-start(f32[128,4,272]{2,1,0:T(4,128)} %copy.50), calls=%async_computation.1 | async-start | bytes 1572864 | tf_op jit(solution)/shard_map/all_to_all | solution.py:84
  80.9 30.2 %all-to-all-start.2 = ((f32[128,4,272]{2,1,0:T(4,128)}), f32[128,4,272]{2,1,0:T(4,128)S(1)}, u32[]{:S(2)}, u32[]{:S(2)}) async-start(f32[128,4,272]{2,1,0:T(4,128)} %copy.53), calls=%async_computation.2 | async-start | bytes 1572864 | tf_op jit(solution)/shard_map/all_to_all | solution.py:85
  87.7 23.4 %copy-start.1 = (f32[2,256,272]{1,2,0:T(8,128)}, f32[2,256,272]{1,2,0:T(8,128)S(1)}, u32[]{:S(2)}) copy-start(f32[2,256,272]{1,2,0:T(8,128)S(1)} %copy.52) | copy-start | bytes 1671172
  113.6 1.6 copy-start.2
  121.1 27.6 %all-to-all-start.3 = ((f32[2,256,256]{2,0,1:T(2,128)}), f32[2,256,256]{2,0,1:T(2,128)S(1)}, u32[]{:S(2)}, u32[]{:S(2)}) async-start(f32[2,256,256]{2,0,1:T(2,128)} %copy.58), calls=%async_computation.3 | async-start | bytes 1048576 | tf_op jit(solution)/shard_map/all_to_all | solution.py:91
  148.7 25.5 %all-to-all-start.4 = ((f32[2,256,256]{2,0,1:T(2,128)}), f32[2,256,256]{2,0,1:T(2,128)S(1)}, u32[]{:S(2)}, u32[]{:S(2)}) async-start(f32[2,256,256]{2,0,1:T(2,128)} %copy.61), calls=%async_computation.4 | async-start | bytes 1048576 | tf_op jit(solution)/shard_map/all_to_all | solution.py:92
  155.1 78.2 %reduce-scatter.2.cloned.1.call-start = ((), (), s32[]{:S(2)}) async-start(), calls=%async_computation.7 | async-start | bytes 1179648 | tf_op jit(solution)/shard_map/reduce_scatter | solution.py:100
  176.0 20.3 %copy-start.3 = (bf16[256,256]{1,0:T(8,128)(2,1)S(1)}, bf16[256,256]{1,0:T(8,128)(2,1)}, u32[]{:S(2)}) copy-start(bf16[256,256]{1,0:T(8,128)(2,1)} %param.8) | copy-start | bytes 393220
  176.0 20.3 %copy-start.4 = (bf16[256,256]{1,0:T(8,128)(2,1)S(1)}, bf16[256,256]{1,0:T(8,128)(2,1)}, u32[]{:S(2)}) copy-start(bf16[256,256]{1,0:T(8,128)(2,1)} %param.6) | copy-start | bytes 393220
  176.0 20.3 %copy-start.5 = (bf16[256,256]{1,0:T(8,128)(2,1)S(1)}, bf16[256,256]{1,0:T(8,128)(2,1)}, u32[]{:S(2)}) copy-start(bf16[256,256]{1,0:T(8,128)(2,1)} %param.7) | copy-start | bytes 393220
  176.0 20.3 %copy-start.6 = (f32[256]{0:T(256)S(1)}, f32[256]{0:T(256)}, u32[]{:S(2)}) copy-start(f32[256]{0:T(256)} %param.10) | copy-start | bytes 3076
Sparse Core Ops, SparseCore 0:
  197.9 35.3 reduce-scatter.1
where the time goes:
time: 245 us; the launch traced here: 240 us
  waiting for transfers between devices  131 us (53%)
  starting transfers between devices  45.9 us (19%)
  blocking collectives  20 us (8%)
  matrix products  17.6 us (7%)
  between operations  13.7 us (6%)
  local copies, waits for them, and re-layouts  9.07 us (4%)
  other arithmetic  2.6 us (1%)
    reduce_scatter x1, waiting for transfers between devices, on_device(): lax.psum_scatter(partial_value.astype(jnp.bfloat16), 'tensor', scatter_di...  35.5 us
    all_to_all x1, waiting for transfers between devices, on_device(): lax.all_to_all(real, 'context', split_axis=0, concat_axis=1, tiled=True)  24.4 us
    all_to_all x1, waiting for transfers between devices, on_device(): lax.all_to_all(imag, 'context', split_axis=0, concat_axis=1, tiled=True)  21.8 us
    all_to_all x1, blocking collectives, on_device(): lax.all_to_all(pieces, 'context', split_axis=0, concat_axis=1, tiled=True)  20 us
    all_to_all x1, waiting for transfers between devices, on_device(): lax.all_to_all(imag, 'context', split_axis=1, concat_axis=0, tiled=True)  18.8 us
    all_to_all x1, starting transfers between devices, on_device(): lax.all_to_all(signal, 'context', split_axis=1, concat_axis=0, tiled=True)  17.6 us
    all_to_all x1, waiting for transfers between devices, on_device(): lax.all_to_all(signal, 'context', split_axis=1, concat_axis=0, tiled=True)  15.9 us
    all_to_all x1, waiting for transfers between devices, on_device(): lax.all_to_all(real, 'context', split_axis=1, concat_axis=0, tiled=True)  14.9 us
  transfers between devices with their start and end apart: 6, of which 6 were waited for; matrix products, arithmetic and copies ran while one was open for 3% of the time, Pallas kernels for 0%

commit v1 on v0

v1 whole, which is shorter than its diff:
```python
import jax
import jax.numpy as jnp
from jax import lax
from jax.experimental import pallas as pl
from jax.experimental.pallas import tpu as pltpu
from jax.sharding import PartitionSpec as P

BLOCK = 128
SLOTS = 16
F32 = jnp.float32
BF16 = jnp.bfloat16


def iota(shape, axis):
    return lax.broadcasted_iota(jnp.int32, shape, axis)


def nt_dot(a, b):
    return lax.dot_general(a, b, (((1,), (1,)), ((), ())), preferred_element_type=F32)


def pack_kernel(in_gate_ref, values_ref, filters_ref, out_ref):
    rows, width = in_gate_ref.shape
    groups = filters_ref.shape[1]
    peers = out_ref.shape[0] // SLOTS
    chans = width // peers
    mixed = (in_gate_ref[...].astype(F32) * values_ref[...].astype(F32)).astype(BF16)
    filters = filters_ref[...].astype(BF16)
    total = None
    for b in range(rows // BLOCK):
        row, col = iota((peers * SLOTS, width), 0), iota((peers * SLOTS, width), 1)
        slot = row % SLOTS
        pick = (slot // chans == b) & ((row // SLOTS) * chans + slot % chans == col)
        part = nt_dot(pick.astype(F32).astype(BF16), mixed[b * BLOCK : (b + 1) * BLOCK])
        row, col = iota((peers * SLOTS, groups), 0), iota((peers * SLOTS, groups), 1)
        pick = (row % SLOTS == 8 + b) & (row // (SLOTS * peers // groups) == col)
        part += nt_dot(pick.astype(F32).astype(BF16), filters[b * BLOCK : (b + 1) * BLOCK])
        total = part if total is None else total + part
    out_ref[...] = total.astype(BF16)


def conv_kernel(in_ref, out_ref, lhs_ref, acc_ref, tap_ref):
    peers = in_ref.shape[0] // SLOTS
    blocks = 2 * peers
    rows = 4 * blocks
    half = blocks // 2
    received = in_ref[...].astype(F32).reshape(peers, 2, 8, BLOCK)
    x = received[:, 0].reshape(rows, BLOCK)
    tap_ref[...] = received[:, 1].reshape(peers * 8, BLOCK)
    for m in range(4):
        moved = x if m == 0 else jnp.concatenate([jnp.zeros((4 * m, BLOCK), F32), x[: rows - 4 * m]], axis=0)
        lhs_ref[:, m * BLOCK : (m + 1) * BLOCK] = moved.astype(BF16)
    acc_ref[...] = jnp.zeros_like(acc_ref)
    keep = iota((BLOCK, BLOCK), 1) >= iota((BLOCK, BLOCK), 0)

    def turned(block):
        if block < 0:
            return jnp.zeros((BLOCK, BLOCK), F32)
        place = (block // 2) * 8 + block % 2
        taps = jnp.broadcast_to(tap_ref[place : place + 1, :], (BLOCK, BLOCK))
        return pltpu.roll(taps, 0, 1, stride=1, stride_axis=0)

    last = {0: turned(-1), half: turned(half - 1)}
    for q in range(half // 4):
        sides = []
        for base in (0, half):
            stack = []
            for m in range(4):
                now = turned(base + 4 * q + m)
                stack.append(jnp.where(keep, now, last[base]).astype(BF16))
                last[base] = now
            sides.append(jnp.concatenate(stack, axis=0))
        near = 16 * q
        both = jnp.concatenate(sides, axis=1)
        mid = rows // 2
        acc_ref[near:mid, :] += jnp.dot(lhs_ref[: mid - near, :], both, preferred_element_type=F32)
        acc_ref[mid:, :BLOCK] += jnp.dot(lhs_ref[mid - near : rows - near, :], sides[0], preferred_element_type=F32)
    out_ref[: rows // 2, :] = acc_ref[: rows // 2, :BLOCK].astype(BF16)
    out_ref[rows // 2 :, :] = (acc_ref[rows // 2 :, :BLOCK] + acc_ref[: rows // 2, BLOCK:]).astype(BF16)


def project_kernel(conv_ref, in_gate_ref, values_ref, out_gate_ref, skip_ref, projection_ref, out_ref):
    rows, width = in_gate_ref.shape
    received = conv_ref[...].astype(F32).T.astype(BF16)
    parts = []
    for b in range(rows // BLOCK):
        row, col = iota((2 * width, width), 0), iota((2 * width, width), 1)
        pick = (row % 8 // 4 == b) & (row // 8 * 4 + row % 4 == col)
        parts.append(jnp.dot(received, pick.astype(F32).astype(BF16), preferred_element_type=F32))
    conv = jnp.concatenate(parts, axis=0)
    mixed = in_gate_ref[...].astype(F32) * values_ref[...].astype(F32)
    combined = conv + skip_ref[...] * mixed
    gated = (combined * out_gate_ref[...].astype(F32)).astype(BF16)
    for k in range(out_ref.shape[0]):
        out_ref[k] = jnp.dot(
            gated, projection_ref[:, k * width : (k + 1) * width], preferred_element_type=F32
        ).astype(BF16)


def sum_kernel(parts_ref, out_ref):
    total = parts_ref[0].astype(F32)
    for k in range(1, parts_ref.shape[0]):
        total += parts_ref[k].astype(F32)
    out_ref[...] = total.astype(BF16)


def call(kernel, shape, *args, scratch=()):
    return pl.pallas_call(
        kernel,
        out_shape=jax.ShapeDtypeStruct(shape, BF16),
        scratch_shapes=scratch,
        compiler_params=pltpu.CompilerParams(vmem_limit_bytes=32 * 1024 * 1024),
    )(*args)


def on_device(in_gate, out_gate, values, long_filters, skip_gain, projection):
    rows, width = in_gate.shape
    contexts = lax.axis_size("context")
    tensors = lax.axis_size("tensor")
    sent = call(pack_kernel, (contexts * SLOTS, BLOCK), in_gate, values, long_filters)
    held = lax.all_to_all(sent.reshape(contexts, SLOTS, BLOCK), "context", 0, 0, tiled=True)
    conv = call(
        conv_kernel,
        (contexts * 8, BLOCK),
        held.reshape(contexts * SLOTS, BLOCK),
        scratch=[
            pltpu.VMEM((contexts * 8, 4 * BLOCK), BF16),
            pltpu.VMEM((contexts * 8, 2 * BLOCK), F32),
            pltpu.VMEM((contexts * 8, BLOCK), F32),
        ],
    )
    back = lax.all_to_all(conv.reshape(contexts, 8, BLOCK), "context", 0, 0, tiled=True)
    partial = call(
        project_kernel,
        (tensors, rows, width),
        back.reshape(contexts * 8, BLOCK),
        in_gate,
        values,
        out_gate,
        skip_gain[None, :],
        projection,
    )
    shares = lax.all_to_all(partial, "tensor", 0, 0, tiled=True)
    return call(sum_kernel, (rows, width), shares)


def solution(mesh):
    return jax.shard_map(
        on_device,
        mesh=mesh,
        in_specs=(
            P("context", "tensor"),
            P("context", "tensor"),
            P("context", "tensor"),
            P("context", "tensor"),
            P("tensor"),
            P("tensor", None),
        ),
        out_specs=P("context", "tensor"),
        check_vma=False,
    )
```

time: 245 us -> 76 us (0.31); the launches traced: 240 us -> 75.7 us
  waiting for transfers between devices: 131 us -> 0 us
  blocking collectives: 20 us -> 68.8 us
  starting transfers between devices: 45.9 us -> 0 us
  matrix products: 17.6 us -> 0 us
  between operations: 13.7 us -> 0.05 us
  local copies, waits for them, and re-layouts: 9.07 us -> 2.5 us
  Pallas kernels: 0 us -> 4.32 us
  other arithmetic: 2.6 us -> 0 us
    all_to_all x5 -> x0, waiting for transfers between devices: 95.7 us -> none  [the longest x1 24.4 us: on_device(): lax.all_to_all(real, 'context', split_axis=0, concat_axis=1, tiled=True)]
    all_to_all x1 -> x3, blocking collectives: 20 us -> 68.8 us  [the longest x1 31.2 us: on_device(): lax.all_to_all(sent.reshape(contexts, SLOTS, BLOCK), 'context', 0, 0, til...]
    all_to_all x5 -> x0, starting transfers between devices: 45.9 us -> none  [the longest x1 17.6 us: on_device(): lax.all_to_all(signal, 'context', split_axis=1, concat_axis=0, tiled=True)]
    reduce_scatter x1 -> x0, waiting for transfers between devices: 35.5 us -> none  [on_device(): lax.psum_scatter(partial_value.astype(jnp.bfloat16), 'tensor', scatter_di...]
    dot_general x13 -> x0, matrix products: 17.6 us -> none  [the longest x2 3.17 us: inner_transform(): jnp.einsum('rm,emk->erk', sine, imag, precision=HIGHEST)]
    pallas_call x0 -> x4, Pallas kernels: none -> 4.32 us  [call(): pl.pallas_call(kernel, out_shape=jax.ShapeDtypeStruct(shape, BF16), scrat...]
  transfers between devices with their start and end apart: 6 -> 0, of which waited for: 6 -> 0; matrix products, arithmetic and copies ran while one was open for 3% -> 0% of each run, Pallas kernels for 0% -> 0%
where the time goes in v1:
time: 76 us; the launch traced here: 75.7 us
  blocking collectives  68.8 us (91%)
  Pallas kernels  4.32 us (6%)
  local copies, waits for them, and re-layouts  2.5 us (3%)
    all_to_all x1, blocking collectives, on_device(): lax.all_to_all(sent.reshape(contexts, SLOTS, BLOCK), 'context', 0, 0, til...  31.2 us
    all_to_all x1, blocking collectives, on_device(): lax.all_to_all(conv.reshape(contexts, 8, BLOCK), 'context', 0, 0, tiled=T...  18.9 us
    all_to_all x1, blocking collectives, on_device(): shares = lax.all_to_all(partial, 'tensor', 0, 0, tiled=True)  18.7 us
    pallas_call x4, Pallas kernels, call(): pl.pallas_call(kernel, out_shape=jax.ShapeDtypeStruct(shape, BF16), scrat...  4.32 us
    unnamed x13, local copies, waits for them, and re-layouts  2.5 us

profile of v1, /device:TPU:1, one launch (start us, length us, event | category | flops | bytes accessed | tf_op | source)
XLA Modules:
  0.0 75.7 jit_solution(4047126323939427564)
XLA Ops:
  0.0 0.0 copy-start.1
  0.0 0.0 copy-start
  0.0 0.9 %copy.7.filters_ref = f32[256,16]{1,0:T(8,128)S(1)} copy(f32[256,16]{0,1:T(8,128)} %param.9) | data formatting | bytes 32768 | tf_op args[3]
  0.9 0.0 copy-done.1
  0.9 0.0 copy-start.2
  0.9 0.9 %copy-done.2 = bf16[256,256]{1,0:T(8,128)(2,1)S(1)} copy-done((bf16[256,256]{1,0:T(8,128)(2,1)S(1)}, bf16[256,256]{1,0:T(8,128)(2,1)}, u32[]{:S(2)}) %copy-start.2) | copy-done | bytes 131096
  1.8 0.6 shard_map.64
  2.4 31.2 %all_to_all.15 = bf16[64,16,128]{2,1,0:T(8,128)(2,1)S(1)} all-to-all(bf16[64,16,128]{2,1,0:T(8,128)(2,1)S(1)} %bitcast.5), channel_id=1, replica_groups=mesh['context'=64,'tensor'=8] {'context'}, dimensions={0} | all-to-all | bytes 524288 | tf_op jit(solution)/shard_map/all_to_all | solution.py:121
  33.6 2.2 %shard_map.65 = bf16[512,128]{1,0:T(8,128)(2,1)S(1)} custom-call(bf16[1024,128]{1,0:T(8,128)(2,1)S(1)} %bitcast.6), custom_call_target="tpu_custom_call" | custom-call | tf_op jit(solution)/shard_map/pallas_call | solution.py:108
  35.9 0.0 copy-start.3
  35.9 0.0 copy-start.4
  35.9 18.9 %all_to_all.16 = bf16[64,8,128]{2,1,0:T(8,128)(2,1)S(1)} all-to-all(bf16[64,8,128]{2,1,0:T(8,128)(2,1)S(1)} %bitcast.7), channel_id=1, replica_groups=mesh['context'=64,'tensor'=8] {'context'}, dimensions={0} | all-to-all | bytes 262144 | tf_op jit(solution)/shard_map/all_to_all | solution.py:132
  54.8 0.0 copy-start.5
  54.8 0.0 copy-done
  54.8 0.0 copy-done.3
  54.8 0.0 copy-done.4
  54.8 0.7 copy-done.5
  55.5 0.7 shard_map.66
  56.2 18.7 %all_to_all.17.parts_ref = bf16[8,256,256]{2,1,0:T(8,128)(2,1)S(1)} all-to-all(bf16[8,256,256]{2,1,0:T(8,128)(2,1)S(1)} %shard_map.66), channel_id=1, replica_groups=mesh['context'=64,'tensor'=8] {'tensor'}, dimensions={0} | all-to-all | bytes 2097152 | tf_op jit(solution)/shard_map/all_to_all | solution.py:143
  74.9 0.8 %shard_map.67 = bf16[256,256]{1,0:T(8,128)(2,1)} custom-call(bf16[8,256,256]{2,1,0:T(8,128)(2,1)S(1)} %all_to_all.17.parts_ref), custom_call_target="tpu_custom_call" | custom-call | tf_op jit(solution)/shard_map/pallas_call | solution.py:108
Async XLA Ops:
  0.0 0.9 %copy-start.1 = (bf16[256,256]{1,0:T(8,128)(2,1)S(1)}, bf16[256,256]{1,0:T(8,128)(2,1)}, u32[]{:S(2)}) copy-start(bf16[256,256]{1,0:T(8,128)(2,1)} %in_gate_ref.3) | copy-start | bytes 393220
  0.0 54.8 %copy-start = (bf16[256,2048]{1,0:T(8,128)(2,1)S(1)}, bf16[256,2048]{1,0:T(8,128)(2,1)}, u32[]{:S(2)}) copy-start(bf16[256,2048]{1,0:T(8,128)(2,1)} %projection_ref.1) | copy-start | bytes 3145732
  0.9 0.9 %copy-start.2 = (bf16[256,256]{1,0:T(8,128)(2,1)S(1)}, bf16[256,256]{1,0:T(8,128)(2,1)}, u32[]{:S(2)}) copy-start(bf16[256,256]{1,0:T(8,128)(2,1)} %values_ref.3) | copy-start | bytes 393220
  35.9 19.0 %copy-start.3 = (bf16[256,256]{1,0:T(8,128)(2,1)S(1)}, bf16[256,256]{1,0:T(8,128)(2,1)}, u32[]{:S(2)}) copy-start(bf16[256,256]{1,0:T(8,128)(2,1)} %values_ref.3) | copy-start | bytes 393220
  35.9 19.0 %copy-start.4 = (bf16[256,256]{1,0:T(8,128)(2,1)S(1)}, bf16[256,256]{1,0:T(8,128)(2,1)}, u32[]{:S(2)}) copy-start(bf16[256,256]{1,0:T(8,128)(2,1)} %out_gate_ref.1) | copy-start | bytes 393220
  54.8 0.7 copy-start.5

commit v2 on v1

--- a/solution.py
+++ b/solution.py
@@ -6,7 +6,7 @@
 from jax.sharding import PartitionSpec as P
 
 BLOCK = 128
-SLOTS = 16
+SLOTS = 10
 F32 = jnp.float32
 BF16 = jnp.bfloat16
 
@@ -19,24 +19,33 @@
     return lax.dot_general(a, b, (((1,), (1,)), ((), ())), preferred_element_type=F32)
 
 
-def pack_kernel(in_gate_ref, values_ref, filters_ref, out_ref):
+def pack_kernel(*refs):
+    sources, (out_ref, direct_ref, out_gate_ref), refs = refs[:5], refs[5:8], refs[8:]
+    in_gate_ref, values_ref, filters_ref, skip_ref, rows_ref, sems = refs
+    targets = (in_gate_ref, values_ref, filters_ref, skip_ref, out_gate_ref)
+    moves = [pltpu.make_async_copy(sources[n], targets[n], sems.at[n]) for n in range(5)]
+    for move in moves:
+        move.start()
     rows, width = in_gate_ref.shape
-    groups = filters_ref.shape[1]
+    groups = filters_ref.shape[0]
     peers = out_ref.shape[0] // SLOTS
     chans = width // peers
-    mixed = (in_gate_ref[...].astype(F32) * values_ref[...].astype(F32)).astype(BF16)
-    filters = filters_ref[...].astype(BF16)
-    total = None
-    for b in range(rows // BLOCK):
-        row, col = iota((peers * SLOTS, width), 0), iota((peers * SLOTS, width), 1)
-        slot = row % SLOTS
-        pick = (slot // chans == b) & ((row // SLOTS) * chans + slot % chans == col)
-        part = nt_dot(pick.astype(F32).astype(BF16), mixed[b * BLOCK : (b + 1) * BLOCK])
-        row, col = iota((peers * SLOTS, groups), 0), iota((peers * SLOTS, groups), 1)
-        pick = (row % SLOTS == 8 + b) & (row // (SLOTS * peers // groups) == col)
-        part += nt_dot(pick.astype(F32).astype(BF16), filters[b * BLOCK : (b + 1) * BLOCK])
-        total = part if total is None else total + part
-    out_ref[...] = total.astype(BF16)
+    row, col = iota((peers * 8, width), 0), iota((peers * 8, width), 1)
+    picks = [
+        ((row % 8 // chans == b) & (row // 8 * chans + row % chans == col)).astype(F32).astype(BF16) for b in range(2)
+    ]
+    for move in moves:
+        move.wait()
+    products = in_gate_ref[...].astype(F32) * values_ref[...].astype(F32)
+    direct_ref[...] = skip_ref[...] * products
+    mixed = products.astype(BF16)
+    sent = sum(nt_dot(picks[b], mixed[b * BLOCK : (b + 1) * BLOCK]) for b in range(2))
+    for j in range(peers):
+        rows_ref[j * SLOTS : j * SLOTS + 8, :] = sent[j * 8 : j * 8 + 8]
+        g = j // (peers // groups)
+        for b in range(2):
+            rows_ref[j * SLOTS + 8 + b : j * SLOTS + 9 + b, :] = filters_ref[g : g + 1, b * BLOCK : (b + 1) * BLOCK]
+    out_ref[...] = rows_ref[...].astype(BF16)
 
 
 def conv_kernel(in_ref, out_ref, lhs_ref, acc_ref, tap_ref):
@@ -44,9 +53,8 @@
     blocks = 2 * peers
     rows = 4 * blocks
     half = blocks // 2
-    received = in_ref[...].astype(F32).reshape(peers, 2, 8, BLOCK)
-    x = received[:, 0].reshape(rows, BLOCK)
-    tap_ref[...] = received[:, 1].reshape(peers * 8, BLOCK)
+    tap_ref[...] = in_ref[...].astype(F32)
+    x = jnp.concatenate([tap_ref[k * SLOTS : k * SLOTS + 8, :] for k in range(peers)], axis=0)
     for m in range(4):
         moved = x if m == 0 else jnp.concatenate([jnp.zeros((4 * m, BLOCK), F32), x[: rows - 4 * m]], axis=0)
         lhs_ref[:, m * BLOCK : (m + 1) * BLOCK] = moved.astype(BF16)
@@ -56,7 +64,7 @@
     def turned(block):
         if block < 0:
             return jnp.zeros((BLOCK, BLOCK), F32)
-        place = (block // 2) * 8 + block % 2
+        place = (block // 2) * SLOTS + 8 + block % 2
         taps = jnp.broadcast_to(tap_ref[place : place + 1, :], (BLOCK, BLOCK))
         return pltpu.roll(taps, 0, 1, stride=1, stride_axis=0)
 
@@ -79,8 +87,8 @@
     out_ref[rows // 2 :, :] = (acc_ref[rows // 2 :, :BLOCK] + acc_ref[: rows // 2, BLOCK:]).astype(BF16)
 
 
-def project_kernel(conv_ref, in_gate_ref, values_ref, out_gate_ref, skip_ref, projection_ref, out_ref):
-    rows, width = in_gate_ref.shape
+def project_kernel(conv_ref, direct_ref, out_gate_ref, projection_ref, out_ref):
+    rows, width = direct_ref.shape
     received = conv_ref[...].astype(F32).T.astype(BF16)
     parts = []
     for b in range(rows // BLOCK):
@@ -88,9 +96,7 @@
         pick = (row % 8 // 4 == b) & (row // 8 * 4 + row % 4 == col)
         parts.append(jnp.dot(received, pick.astype(F32).astype(BF16), preferred_element_type=F32))
     conv = jnp.concatenate(parts, axis=0)
-    mixed = in_gate_ref[...].astype(F32) * values_ref[...].astype(F32)
-    combined = conv + skip_ref[...] * mixed
-    gated = (combined * out_gate_ref[...].astype(F32)).astype(BF16)
+    gated = ((conv + direct_ref[...]) * out_gate_ref[...].astype(F32)).astype(BF16)
     for k in range(out_ref.shape[0]):
         out_ref[k] = jnp.dot(
             gated, projection_ref[:, k * width : (k + 1) * width], preferred_element_type=F32
@@ -117,8 +123,26 @@
     rows, width = in_gate.shape
     contexts = lax.axis_size("context")
     tensors = lax.axis_size("tensor")
-    sent = call(pack_kernel, (contexts * SLOTS, BLOCK), in_gate, values, long_filters)
-    held = lax.all_to_all(sent.reshape(contexts, SLOTS, BLOCK), "context", 0, 0, tiled=True)
+    args = (in_gate, values, long_filters.T, skip_gain[None, :], out_gate)
+    sent, direct, out_gate = pl.pallas_call(
+        pack_kernel,
+        in_specs=[pl.BlockSpec(memory_space=pltpu.HBM)] * len(args),
+        out_shape=[
+            jax.ShapeDtypeStruct((contexts * SLOTS, BLOCK), BF16),
+            jax.ShapeDtypeStruct((rows, width), F32),
+            jax.ShapeDtypeStruct((rows, width), BF16),
+        ],
+        scratch_shapes=[
+            pltpu.VMEM((rows, width), BF16),
+            pltpu.VMEM((rows, width), BF16),
+            pltpu.VMEM((long_filters.shape[1], rows), F32),
+            pltpu.VMEM((1, width), F32),
+            pltpu.VMEM((contexts * SLOTS, BLOCK), F32),
+            pltpu.SemaphoreType.DMA((len(args),)),
+        ],
+        compiler_params=pltpu.CompilerParams(vmem_limit_bytes=32 * 1024 * 1024),
+    )(*(pltpu.with_memory_space_constraint(a, pltpu.HBM) for a in args))
+    held = lax.all_to_all(sent.reshape(contexts * SLOTS // 2, 2, BLOCK), "context", 0, 0, tiled=True)
     conv = call(
         conv_kernel,
         (contexts * 8, BLOCK),
@@ -126,7 +150,7 @@
         scratch=[
             pltpu.VMEM((contexts * 8, 4 * BLOCK), BF16),
             pltpu.VMEM((contexts * 8, 2 * BLOCK), F32),
-            pltpu.VMEM((contexts * 8, BLOCK), F32),
+            pltpu.VMEM((contexts * SLOTS, BLOCK), F32),
         ],
     )
     back = lax.all_to_all(conv.reshape(contexts, 8, BLOCK), "context", 0, 0, tiled=True)
@@ -134,10 +158,8 @@
         project_kernel,
         (tensors, rows, width),
         back.reshape(contexts * 8, BLOCK),
-        in_gate,
-        values,
+        direct,
         out_gate,
-        skip_gain[None, :],
         projection,
     )
     shares = lax.all_to_all(partial, "tensor", 0, 0, tiled=True)

time: 76 us -> 71.8 us (0.945)
  blocking collectives: 68.8 us -> 66.3 us
  local copies, waits for them, and re-layouts: 2.5 us -> 0.01 us
  Pallas kernels: 4.32 us -> 5.27 us
    unnamed x13 -> x2, local copies, waits for them, and re-layouts: 2.5 us -> 0.01 us
    pallas_call x0 -> x1, Pallas kernels: none -> 1.56 us  [on_device(): pl.pallas_call(pack_kernel, in_specs=[pl.BlockSpec(memory_space=pltpu.HBM...]
    all_to_all x1, blocking collectives: 18.9 us -> 17.5 us  [on_device(): lax.all_to_all(conv.reshape(contexts, 8, BLOCK), 'context', 0, 0, tiled=T...]
    all_to_all x1, blocking collectives: 31.2 us -> 30.2 us  [on_device(): lax.all_to_all(sent.reshape(contexts * SLOTS // 2, 2, BLOCK), 'context',...]
    pallas_call x4 -> x3, Pallas kernels: 4.32 us -> 3.71 us  [call(): pl.pallas_call(kernel, out_shape=jax.ShapeDtypeStruct(shape, BF16), scrat...]
where the time goes in v2:
time: 71.8 us; the launch traced here: 71.6 us
  blocking collectives  66.3 us (92%)
  Pallas kernels  5.27 us (7%)
    all_to_all x1, blocking collectives, on_device(): lax.all_to_all(sent.reshape(contexts * SLOTS // 2, 2, BLOCK), 'context',...  30.2 us
    all_to_all x1, blocking collectives, on_device(): shares = lax.all_to_all(partial, 'tensor', 0, 0, tiled=True)  18.6 us
    all_to_all x1, blocking collectives, on_device(): lax.all_to_all(conv.reshape(contexts, 8, BLOCK), 'context', 0, 0, tiled=T...  17.5 us
    pallas_call x3, Pallas kernels, call(): pl.pallas_call(kernel, out_shape=jax.ShapeDtypeStruct(shape, BF16), scrat...  3.71 us
    pallas_call x1, Pallas kernels, on_device(): pl.pallas_call(pack_kernel, in_specs=[pl.BlockSpec(memory_space=pltpu.HBM...  1.56 us

profile of v2, /device:TPU:1, one launch (start us, length us, event | category | flops | bytes accessed | tf_op | source)
XLA Modules:
  0.0 71.6 jit_solution(604277112252920306)
XLA Ops:
  0.0 0.0 copy-start
  0.0 1.6 %shard_map.64 = (bf16[640,128]{1,0:T(8,128)(2,1)S(1)}, f32[256,256]{1,0:T(8,128)S(1)}, bf16[256,256]{1,0:T(8,128)(2,1)S(1)}) custom-call(bf16[256,256]{1,0:T(8,128)(2,1)} %refs_0_.1, bf16[256,256]{1,0:T(8,128)(2,1)} %refs_1_.1, f32[16,256]{1,0:T(8,128)} %bitcast.10, f32[1,256]{1,0:T(1,128)} %bitcast.11, bf16[256,256]{1,0:T(8,128)(2,1)} %refs_4_.1), custom_call_target="tpu_custom_call" | custom-call | tf_op jit(solution)/shard_map/pallas_call | solution.py:127
  1.6 30.2 %all_to_all.15 = bf16[320,2,128]{2,1,0:T(2,128)(2,1)S(1)} all-to-all(bf16[320,2,128]{2,1,0:T(2,128)(2,1)S(1)} %bitcast.9), channel_id=1, replica_groups=mesh['context'=64,'tensor'=8] {'context'}, dimensions={0} | all-to-all | bytes 327680 | tf_op jit(solution)/shard_map/all_to_all | solution.py:145
  31.7 2.2 %shard_map.65 = bf16[512,128]{1,0:T(8,128)(2,1)S(1)} custom-call(bf16[640,128]{1,0:T(8,128)(2,1)S(1)} %bitcast.6), custom_call_target="tpu_custom_call" | custom-call | tf_op jit(solution)/shard_map/pallas_call | solution.py:114
  33.9 17.5 %all_to_all.16 = bf16[64,8,128]{2,1,0:T(8,128)(2,1)S(1)} all-to-all(bf16[64,8,128]{2,1,0:T(8,128)(2,1)S(1)} %bitcast.8), channel_id=1, replica_groups=mesh['context'=64,'tensor'=8] {'context'}, dimensions={0} | all-to-all | bytes 262144 | tf_op jit(solution)/shard_map/all_to_all | solution.py:156
  51.5 0.0 copy-done
  51.5 0.7 %shard_map.66 = bf16[8,256,256]{2,1,0:T(8,128)(2,1)S(1)} custom-call(bf16[512,128]{1,0:T(8,128)(2,1)S(1)} %bitcast.7, f32[256,256]{1,0:T(8,128)S(1)} %get-tuple-element.9.direct_ref, bf16[256,256]{1,0:T(8,128)(2,1)S(1)} %get-tuple-element.10.out_gate_ref, bf16[256,2048]{1,0:T(8,128)(2,1)S(1)} %copy-done), custom_call_target="tpu_custom_call" | custom-call | tf_op jit(solution)/shard_map/pallas_call | solution.py:114
  52.2 18.6 %all_to_all.17.parts_ref = bf16[8,256,256]{2,1,0:T(8,128)(2,1)S(1)} all-to-all(bf16[8,256,256]{2,1,0:T(8,128)(2,1)S(1)} %shard_map.66), channel_id=1, replica_groups=mesh['context'=64,'tensor'=8] {'tensor'}, dimensions={0} | all-to-all | bytes 2097152 | tf_op jit(solution)/shard_map/all_to_all | solution.py:165
  70.8 0.8 %shard_map.67 = bf16[256,256]{1,0:T(8,128)(2,1)} custom-call(bf16[8,256,256]{2,1,0:T(8,128)(2,1)S(1)} %all_to_all.17.parts_ref), custom_call_target="tpu_custom_call" | custom-call | tf_op jit(solution)/shard_map/pallas_call | solution.py:114
Async XLA Ops:
  0.0 51.5 %copy-start = (bf16[256,2048]{1,0:T(8,128)(2,1)S(1)}, bf16[256,2048]{1,0:T(8,128)(2,1)}, u32[]{:S(2)}) copy-start(bf16[256,2048]{1,0:T(8,128)(2,1)} %projection_ref.1) | copy-start | bytes 3145732

commit v3 on v2

v3 whole, which is shorter than its diff:
```python
import jax
import jax.numpy as jnp
from jax import lax
from jax.experimental import pallas as pl
from jax.experimental.pallas import tpu as pltpu
from jax.sharding import Mesh, PartitionSpec as P

BLOCK = 128
SLOTS = 10
TENSOR = ("x_far", "x_near", "y_near")
PAIR = "x_near"
PIECES = 8
SHARE = 16
F32 = jnp.float32
BF16 = jnp.bfloat16


def iota(shape, axis):
    return lax.broadcasted_iota(jnp.int32, shape, axis)


def nt_dot(a, b):
    return lax.dot_general(a, b, (((1,), (1,)), ((), ())), preferred_element_type=F32)


def fold(ref, start, block):
    for k in range(BLOCK // SHARE):
        ref[start : start + SHARE, k * block.shape[1] : (k + 1) * block.shape[1]] = block[k * SHARE : (k + 1) * SHARE]


def unfold(ref, start, width):
    return jnp.concatenate([ref[start : start + SHARE, k * width : (k + 1) * width] for k in range(BLOCK // SHARE)], axis=0)


def pack_kernel(*refs):
    sources, projection, (out_ref, direct_ref, own_gate_ref, leaving_ref), refs = refs[:5], refs[5], refs[6:10], refs[10:]
    in_gate_ref, values_ref, filters_ref, skip_ref, out_gate_ref, rows_ref, sems = refs
    targets = (in_gate_ref, values_ref, filters_ref, skip_ref, out_gate_ref)
    moves = [pltpu.make_async_copy(sources[n], targets[n], sems.at[n]) for n in range(5)]
    for move in moves:
        move.start()
    depth = projection.shape[0]
    share = depth // PIECES
    copied = [
        pltpu.make_async_copy(
            projection.at[n * share : (n + 1) * share], leaving_ref.at[n * share : (n + 1) * share], sems.at[5 + n]
        )
        for n in range(PIECES)
    ]
    for move in copied:
        move.start()
    rows, width = in_gate_ref.shape
    groups = filters_ref.shape[0]
    peers = out_ref.shape[0] // SLOTS
    chans = width // peers
    row, col = iota((peers * 8, width), 0), iota((peers * 8, width), 1)
    picks = [
        ((row % 8 // chans == b) & (row // 8 * chans + row % chans == col)).astype(F32).astype(BF16) for b in range(2)
    ]
    for move in moves:
        move.wait()
    products = in_gate_ref[...].astype(F32) * values_ref[...].astype(F32)
    direct = skip_ref[...] * products
    first = lax.axis_index(PAIR) == 0
    low, high = direct[:BLOCK], direct[BLOCK:]
    direct_ref[...] = jnp.where(first, low, high)
    fold(leaving_ref, depth, jnp.where(first, high, low).astype(BF16))
    low, high = out_gate_ref[:BLOCK].astype(F32), out_gate_ref[BLOCK:].astype(F32)
    own_gate_ref[...] = jnp.where(first, low, high).astype(BF16)
    fold(leaving_ref, depth + SHARE, jnp.where(first, high, low).astype(BF16))
    mixed = products.astype(BF16)
    sent = sum(nt_dot(picks[b], mixed[b * BLOCK : (b + 1) * BLOCK]) for b in range(2))
    for j in range(peers):
        rows_ref[j * SLOTS : j * SLOTS + 8, :] = sent[j * 8 : j * 8 + 8]
        g = j // (peers // groups)
        for b in range(2):
            rows_ref[j * SLOTS + 8 + b : j * SLOTS + 9 + b, :] = filters_ref[g : g + 1, b * BLOCK : (b + 1) * BLOCK]
    out_ref[...] = rows_ref[...].astype(BF16)
    for move in copied:
        move.wait()


def conv_kernel(in_ref, out_ref, lhs_ref, acc_ref, tap_ref):
    peers = in_ref.shape[0] // SLOTS
    blocks = 2 * peers
    rows = 4 * blocks
    tap_ref[...] = in_ref[...].astype(F32)
    x = jnp.concatenate([tap_ref[k * SLOTS : k * SLOTS + 8, :] for k in range(peers)], axis=0)
    for m in range(4):
        moved = x if m == 0 else jnp.concatenate([jnp.zeros((4 * m, BLOCK), F32), x[: rows - 4 * m]], axis=0)
        lhs_ref[:, m * BLOCK : (m + 1) * BLOCK] = moved.astype(BF16)
    acc_ref[...] = jnp.zeros_like(acc_ref)
    keep = iota((BLOCK, BLOCK), 1) >= iota((BLOCK, BLOCK), 0)

    def turned(block):
        if block < 0:
            return jnp.zeros((BLOCK, BLOCK), F32)
        place = (block // 2) * SLOTS + 8 + block % 2
        taps = jnp.broadcast_to(tap_ref[place : place + 1, :], (BLOCK, BLOCK))
        return pltpu.roll(taps, 0, 1, stride=1, stride_axis=0)

    step = blocks // 8
    for first in range(0, blocks, 2 * step):
        last = [turned(first - 1), turned(first + step - 1)]
        for q in range(first, first + step, 4):
            sides = []
            for side in range(2):
                stack = []
                for m in range(4):
                    now = turned(q + side * step + m)
                    stack.append(jnp.where(keep, now, last[side]).astype(BF16))
                    last[side] = now
                sides.append(jnp.concatenate(stack, axis=0))
            both = jnp.concatenate(sides, axis=1)
            acc_ref[4 * q :, :] += jnp.dot(lhs_ref[: rows - 4 * q, :], both, preferred_element_type=F32)
    moved = 4 * step
    out_ref[:moved, :] = acc_ref[:moved, :BLOCK].astype(BF16)
    out_ref[moved:, :] = (acc_ref[moved:, :BLOCK] + acc_ref[: rows - moved, BLOCK:]).astype(BF16)


def project_kernel(conv_ref, direct_ref, own_gate_ref, own_rows_ref, given_ref, out_ref):
    width = direct_ref.shape[1]
    depth = own_rows_ref.shape[0] - 2 * SHARE
    received = conv_ref[...].astype(F32).T.astype(BF16)
    here = lax.axis_index(PAIR)
    gated = []
    for side, direct, gate in (
        (here, direct_ref[...], own_gate_ref[...]),
        (1 - here, unfold(given_ref, depth, width).astype(F32), unfold(given_ref, depth + SHARE, width)),
    ):
        row, col = iota((2 * width, width), 0), iota((2 * width, width), 1)
        pick = (row % 8 // 4 == side) & (row // 8 * 4 + row % 4 == col)
        conv = jnp.dot(received, pick.astype(F32).astype(BF16), preferred_element_type=F32)
        gated.append(((conv + direct) * gate.astype(F32)).astype(BF16))
    for k in range(out_ref.shape[0]):
        total = jnp.dot(gated[0], own_rows_ref[:depth, k * width : (k + 1) * width], preferred_element_type=F32)
        total += jnp.dot(gated[1], given_ref[:depth, k * width : (k + 1) * width], preferred_element_type=F32)
        out_ref[k] = total.astype(BF16)


def sum_kernel(parts_ref, out_ref):
    step = {"x_far": 4, "x_near": 2, "y_near": 1}[PAIR]
    for side in range(2):
        total = None
        for k in range(parts_ref.shape[0]):
            if k // step % 2 == side:
                part = parts_ref[k].astype(F32)
                total = part if total is None else total + part
        out_ref[side * BLOCK : (side + 1) * BLOCK, :] = total.astype(BF16)


def call(kernel, shape, *args, scratch=(), cost=None):
    return pl.pallas_call(
        kernel,
        out_shape=jax.ShapeDtypeStruct(shape, BF16),
        scratch_shapes=scratch,
        cost_estimate=cost,
        compiler_params=pltpu.CompilerParams(vmem_limit_bytes=32 * 1024 * 1024),
    )(*args)


def on_device(in_gate, out_gate, values, long_filters, skip_gain, projection):
    rows, width = in_gate.shape
    contexts = lax.axis_size("context")
    tensors = lax.axis_size(TENSOR)
    args = (in_gate, values, long_filters.T, skip_gain[None, :], out_gate, projection)
    sent, direct, own_gate, leaving = pl.pallas_call(
        pack_kernel,
        in_specs=[pl.BlockSpec(memory_space=pltpu.HBM)] * len(args),
        out_shape=[
            jax.ShapeDtypeStruct((contexts * SLOTS, BLOCK), BF16),
            jax.ShapeDtypeStruct((BLOCK, width), F32),
            jax.ShapeDtypeStruct((BLOCK, width), BF16),
            jax.ShapeDtypeStruct((projection.shape[0] + 2 * SHARE, projection.shape[1]), BF16),
        ],
        scratch_shapes=[
            pltpu.VMEM((rows, width), BF16),
            pltpu.VMEM((rows, width), BF16),
            pltpu.VMEM((long_filters.shape[1], rows), F32),
            pltpu.VMEM((1, width), F32),
            pltpu.VMEM((rows, width), BF16),
            pltpu.VMEM((contexts * SLOTS, BLOCK), F32),
            pltpu.SemaphoreType.DMA((len(args) - 1 + PIECES,)),
        ],
        compiler_params=pltpu.CompilerParams(vmem_limit_bytes=32 * 1024 * 1024),
    )(*(pltpu.with_memory_space_constraint(a, pltpu.HBM) for a in args))
    held = lax.all_to_all(sent.reshape(contexts * SLOTS // 2, 2, BLOCK), "context", 0, 0, tiled=True)
    conv = call(
        conv_kernel,
        (contexts * 8, BLOCK),
        held.reshape(contexts * SLOTS, BLOCK),
        cost=pl.CostEstimate(flops=8000000000, bytes_accessed=300000, transcendentals=0),
        scratch=[
            pltpu.VMEM((contexts * 8, 4 * BLOCK), BF16),
            pltpu.VMEM((contexts * 8, 2 * BLOCK), F32),
            pltpu.VMEM((contexts * SLOTS, BLOCK), F32),
        ],
    )
    given = lax.ppermute(leaving, PAIR, [(0, 1), (1, 0)])
    back = lax.all_to_all(conv.reshape(2 * contexts, 4, BLOCK), ("context", PAIR), 0, 0, tiled=True)
    partial = call(
        project_kernel,
        (tensors, BLOCK, width),
        back.reshape(contexts * 8, BLOCK),
        direct,
        own_gate,
        leaving,
        given,
    )
    shares = lax.all_to_all(partial, TENSOR, 0, 0, tiled=True)
    return call(sum_kernel, (rows, width), shares)


def solution(mesh):
    contexts = mesh.shape["context"]
    fine = Mesh(mesh.devices.reshape(contexts, 2, 2, 2), ("context",) + TENSOR)
    return jax.shard_map(
        on_device,
        mesh=fine,
        in_specs=(
            P("context", TENSOR),
            P("context", TENSOR),
            P("context", TENSOR),
            P("context", TENSOR),
            P(TENSOR),
            P(TENSOR, None),
        ),
        out_specs=P("context", TENSOR),
        check_vma=False,
    )
```

time: 71.8 us -> 69.6 us (0.969)
  blocking collectives: 66.3 us -> 33.2 us
  starting transfers between devices: 0 us -> 20.8 us
  waiting for transfers between devices: 0 us -> 9.64 us
    all_to_all x3 -> x2, blocking collectives: 66.3 us -> 33.2 us  [the longest x1 20.1 us: on_device(): lax.all_to_all(conv.reshape(2 * contexts, 4, BLOCK), ('context', PAIR), 0...]
    all_to_all x0 -> x1, starting transfers between devices: none -> 17.6 us  [on_device(): lax.all_to_all(sent.reshape(contexts * SLOTS // 2, 2, BLOCK), 'context',...]
    all_to_all x0 -> x1, waiting for transfers between devices: none -> 9.63 us  [on_device(): lax.all_to_all(sent.reshape(contexts * SLOTS // 2, 2, BLOCK), 'context',...]
    ppermute x0 -> x1, starting transfers between devices: none -> 3.12 us  [on_device(): given = lax.ppermute(leaving, PAIR, [(0, 1), (1, 0)])]
  transfers between devices with their start and end apart: 0 -> 2, of which waited for: 0 -> 1; matrix products, arithmetic and copies ran while one was open for 0% -> 0% of each run, Pallas kernels for 0% -> 3%
where the time goes in v3:
time: 69.6 us; the launch traced here: 69.3 us
  blocking collectives  33.2 us (48%)
  starting transfers between devices  20.8 us (30%)
  waiting for transfers between devices  9.64 us (14%)
  Pallas kernels  5.72 us (8%)
    all_to_all x1, blocking collectives, on_device(): lax.all_to_all(conv.reshape(2 * contexts, 4, BLOCK), ('context', PAIR), 0...  20.1 us
    all_to_all x1, starting transfers between devices, on_device(): lax.all_to_all(sent.reshape(contexts * SLOTS // 2, 2, BLOCK), 'context',...  17.6 us
    all_to_all x1, blocking collectives, on_device(): shares = lax.all_to_all(partial, TENSOR, 0, 0, tiled=True)  13 us
    all_to_all x1, waiting for transfers between devices, on_device(): lax.all_to_all(sent.reshape(contexts * SLOTS // 2, 2, BLOCK), 'context',...  9.63 us
    pallas_call x3, Pallas kernels, call(): pl.pallas_call(kernel, out_shape=jax.ShapeDtypeStruct(shape, BF16), scrat...  3.47 us
    ppermute x1, starting transfers between devices, on_device(): given = lax.ppermute(leaving, PAIR, [(0, 1), (1, 0)])  3.12 us
    pallas_call x1, Pallas kernels, on_device(): pl.pallas_call(pack_kernel, in_specs=[pl.BlockSpec(memory_space=pltpu.HBM...  2.26 us
  transfers between devices with their start and end apart: 2, of which 1 were waited for; matrix products, arithmetic and copies ran while one was open for 0% of the time, Pallas kernels for 3%

profile of v3, /device:TPU:1, one launch (start us, length us, event | category | flops | bytes accessed | tf_op | source)
XLA Modules:
  0.0 69.3 jit_solution(10272459574171040385)
XLA Ops:
  0.0 2.3 %shard_map.64 = (bf16[640,128]{1,0:T(8,128)(2,1)}, f32[128,256]{1,0:T(8,128)S(1)}, bf16[128,256]{1,0:T(8,128)(2,1)S(1)}, bf16[288,2048]{1,0:T(8,128)(2,1)S(1)}) custom-call(bf16[256,256]{1,0:T(8,128)(2,1)} %refs_0_.1, bf16[256,256]{1,0:T(8,128)(2,1)} %refs_1_.1, f32[16,256]{1,0:T(8,128)} %bitcast.9, f32[1,256]{1,0:T(1,128)} %bitcast.10, ...), custom_call_target="tpu_custom_call" | custom-call | tf_op jit(solution)/shard_map/pallas_call | solution.py:167
  2.3 17.6 %all-to-all-start = ((bf16[320,2,128]{2,1,0:T(2,128)(2,1)}), bf16[320,2,128]{2,1,0:T(2,128)(2,1)S(1)}, u32[]{:S(2)}, u32[]{:S(2)}) async-start(bf16[320,2,128]{2,1,0:T(2,128)(2,1)} %bitcast.2), calls=%async_computation | async-start | bytes 327680 | tf_op jit(solution)/shard_map/all_to_all | solution.py:187
  19.9 3.1 %collective-permute-start = (bf16[288,2048]{1,0:T(8,128)(2,1)S(1)}, bf16[288,2048]{1,0:T(8,128)(2,1)S(1)}, u32[]{:S(2)}, u32[]{:S(2)}) collective-permute-start(bf16[288,2048]{1,0:T(8,128)(2,1)S(1)} %get-tuple-element.12.own_rows_ref), channel_id=1, source_target_pairs={{0,2},{2,0},{1,3},{3,1},{4,6},{6,4},{5,7},{7,5},{8,10},{10,8},{9,1... | collective-permute-start | bytes 3538952 | tf_op jit(solution)/shard_map/ppermute | solution.py:199
  23.0 9.6 %all-to-all-done = bf16[320,2,128]{2,1,0:T(2,128)(2,1)S(1)} async-done(((bf16[320,2,128]{2,1,0:T(2,128)(2,1)}), bf16[320,2,128]{2,1,0:T(2,128)(2,1)S(1)}, u32[]{:S(2)}, u32[]{:S(2)}) %all-to-all-start) | async-done | bytes 163872 | tf_op jit(solution)/shard_map/all_to_all | solution.py:187
  32.7 2.0 %shard_map.65 = bf16[512,128]{1,0:T(8,128)(2,1)S(1)} custom-call(bf16[640,128]{1,0:T(8,128)(2,1)S(1)} %bitcast.7), custom_call_target="tpu_custom_call" | custom-call | flops 8000000000 | bytes 300000 | tf_op jit(solution)/shard_map/pallas_call | solution.py:153
  34.7 20.1 %all_to_all.15 = bf16[128,4,128]{2,1,0:T(4,128)(2,1)S(1)} all-to-all(bf16[128,4,128]{2,1,0:T(4,128)(2,1)S(1)} %bitcast.8), channel_id=1, replica_groups=mesh['context'=64,'x_far'=2,'x_near'=2,'y_near'=2] {'context','x_near'}, dimensions={0} | all-to-all | bytes 262144 | tf_op jit(solution)/shard_map/all_to_all | solution.py:200
  54.8 0.0 collective-permute-done.given_ref
  54.8 0.7 %shard_map.66 = bf16[8,128,256]{2,1,0:T(8,128)(2,1)S(1)} custom-call(bf16[512,128]{1,0:T(8,128)(2,1)S(1)} %bitcast.6, f32[128,256]{1,0:T(8,128)S(1)} %get-tuple-element.10.direct_ref, bf16[128,256]{1,0:T(8,128)(2,1)S(1)} %get-tuple-element.11.own_gate_ref, bf16[288,2048]{1,0:T(8,128)(2,1)S(1)} %get-tuple-element.12.own_rows_ref, ...), custom_call_target="tpu_custom_call" | custom-call | tf_op jit(solution)/shard_map/pallas_call | solution.py:153
  55.6 13.0 %all_to_all.16.parts_ref = bf16[8,128,256]{2,1,0:T(8,128)(2,1)S(1)} all-to-all(bf16[8,128,256]{2,1,0:T(8,128)(2,1)S(1)} %shard_map.66), channel_id=1, replica_groups=mesh['context'=64,'x_far'=2,'x_near'=2,'y_near'=2] {'x_far','x_near','y_..., dimensions={0} | all-to-all | bytes 1048576 | tf_op jit(solution)/shard_map/all_to_all | solution.py:210
  68.6 0.7 %shard_map.67 = bf16[256,256]{1,0:T(8,128)(2,1)} custom-call(bf16[8,128,256]{2,1,0:T(8,128)(2,1)S(1)} %all_to_all.16.parts_ref), custom_call_target="tpu_custom_call" | custom-call | tf_op jit(solution)/shard_map/pallas_call | solution.py:153
Async XLA Ops:
  2.3 30.4 %all-to-all-start = ((bf16[320,2,128]{2,1,0:T(2,128)(2,1)}), bf16[320,2,128]{2,1,0:T(2,128)(2,1)S(1)}, u32[]{:S(2)}, u32[]{:S(2)}) async-start(bf16[320,2,128]{2,1,0:T(2,128)(2,1)} %bitcast.2), calls=%async_computation | async-start | bytes 327680 | tf_op jit(solution)/shard_map/all_to_all | solution.py:187
  19.9 34.9 %collective-permute-start = (bf16[288,2048]{1,0:T(8,128)(2,1)S(1)}, bf16[288,2048]{1,0:T(8,128)(2,1)S(1)}, u32[]{:S(2)}, u32[]{:S(2)}) collective-permute-start(bf16[288,2048]{1,0:T(8,128)(2,1)S(1)} %get-tuple-element.12.own_rows_ref), channel_id=1, source_target_pairs={{0,2},{2,0},{1,3},{3,1},{4,6},{6,4},{5,7},{7,5},{8,10},{10,8},{9,1... | collective-permute-start | bytes 3538952 | tf_op jit(solution)/shard_map/ppermute | solution.py:199

commit v4 on v3

--- a/solution.py
+++ b/solution.py
@@ -7,8 +7,10 @@
 
 BLOCK = 128
 SLOTS = 10
+Y_FAR = 4
+CONTEXT = ("y_far", "line")
 TENSOR = ("x_far", "x_near", "y_near")
-PAIR = "x_near"
+PAIR = "y_near"
 PIECES = 8
 SHARE = 16
 F32 = jnp.float32
@@ -33,20 +35,21 @@
 
 
 def pack_kernel(*refs):
-    sources, projection, (out_ref, direct_ref, own_gate_ref, leaving_ref), refs = refs[:5], refs[5], refs[6:10], refs[10:]
+    sources, projection, outs, refs = refs[:5], refs[5], refs[6:11], refs[11:]
+    out_ref, direct_ref, own_gate_ref, leaving_ref, leaving_back_ref = outs
     in_gate_ref, values_ref, filters_ref, skip_ref, out_gate_ref, rows_ref, sems = refs
     targets = (in_gate_ref, values_ref, filters_ref, skip_ref, out_gate_ref)
     moves = [pltpu.make_async_copy(sources[n], targets[n], sems.at[n]) for n in range(5)]
     for move in moves:
         move.start()
-    depth = projection.shape[0]
-    share = depth // PIECES
-    copied = [
-        pltpu.make_async_copy(
-            projection.at[n * share : (n + 1) * share], leaving_ref.at[n * share : (n + 1) * share], sems.at[5 + n]
-        )
-        for n in range(PIECES)
-    ]
+    depth = projection.shape[0] // 2
+    share = 2 * depth // PIECES
+    copied = []
+    for n in range(PIECES):
+        start = n * share
+        holder, at = (leaving_ref, start) if start < depth else (leaving_back_ref, start - depth)
+        target = holder.at[at : at + share]
+        copied.append(pltpu.make_async_copy(projection.at[start : start + share], target, sems.at[5 + n]))
     for move in copied:
         move.start()
     rows, width = in_gate_ref.shape
@@ -118,23 +121,33 @@
     out_ref[moved:, :] = (acc_ref[moved:, :BLOCK] + acc_ref[: rows - moved, BLOCK:]).astype(BF16)
 
 
-def project_kernel(conv_ref, direct_ref, own_gate_ref, own_rows_ref, given_ref, out_ref):
+def gate_kernel(conv_ref, direct_ref, own_gate_ref, given_ref, out_ref):
     width = direct_ref.shape[1]
-    depth = own_rows_ref.shape[0] - 2 * SHARE
+    depth = given_ref.shape[0] - 2 * SHARE
     received = conv_ref[...].astype(F32).T.astype(BF16)
     here = lax.axis_index(PAIR)
-    gated = []
-    for side, direct, gate in (
-        (here, direct_ref[...], own_gate_ref[...]),
-        (1 - here, unfold(given_ref, depth, width).astype(F32), unfold(given_ref, depth + SHARE, width)),
+    for n, (side, direct, gate) in enumerate(
+        (
+            (here, direct_ref[...], own_gate_ref[...]),
+            (1 - here, unfold(given_ref, depth, width).astype(F32), unfold(given_ref, depth + SHARE, width)),
+        )
     ):
         row, col = iota((2 * width, width), 0), iota((2 * width, width), 1)
         pick = (row % 8 // 4 == side) & (row // 8 * 4 + row % 4 == col)
         conv = jnp.dot(received, pick.astype(F32).astype(BF16), preferred_element_type=F32)
-        gated.append(((conv + direct) * gate.astype(F32)).astype(BF16))
+        out_ref[:, n * width : (n + 1) * width] = ((conv + direct) * gate.astype(F32)).astype(BF16)
+
+
+def project_kernel(gated_ref, own_ref, own_back_ref, given_ref, given_back_ref, out_ref):
+    width = out_ref.shape[2]
+    depth = own_back_ref.shape[0]
+    own_gated, given_gated = gated_ref[:, :width], gated_ref[:, width:]
     for k in range(out_ref.shape[0]):
-        total = jnp.dot(gated[0], own_rows_ref[:depth, k * width : (k + 1) * width], preferred_element_type=F32)
-        total += jnp.dot(gated[1], given_ref[:depth, k * width : (k + 1) * width], preferred_element_type=F32)
+        part = slice(k * width, (k + 1) * width)
+        own = jnp.concatenate([own_ref[:depth, part], own_back_ref[:, part]], axis=0)
+        given = jnp.concatenate([given_ref[:depth, part], given_back_ref[:, part]], axis=0)
+        total = jnp.dot(own_gated, own, preferred_element_type=F32)
+        total += jnp.dot(given_gated, given, preferred_element_type=F32)
         out_ref[k] = total.astype(BF16)
 
 
@@ -161,17 +174,18 @@
 
 def on_device(in_gate, out_gate, values, long_filters, skip_gain, projection):
     rows, width = in_gate.shape
-    contexts = lax.axis_size("context")
+    contexts = lax.axis_size(CONTEXT)
     tensors = lax.axis_size(TENSOR)
     args = (in_gate, values, long_filters.T, skip_gain[None, :], out_gate, projection)
-    sent, direct, own_gate, leaving = pl.pallas_call(
+    sent, direct, own_gate, leaving, leaving_back = pl.pallas_call(
         pack_kernel,
         in_specs=[pl.BlockSpec(memory_space=pltpu.HBM)] * len(args),
         out_shape=[
             jax.ShapeDtypeStruct((contexts * SLOTS, BLOCK), BF16),
             jax.ShapeDtypeStruct((BLOCK, width), F32),
             jax.ShapeDtypeStruct((BLOCK, width), BF16),
-            jax.ShapeDtypeStruct((projection.shape[0] + 2 * SHARE, projection.shape[1]), BF16),
+            jax.ShapeDtypeStruct((projection.shape[0] // 2 + 2 * SHARE, projection.shape[1]), BF16),
+            jax.ShapeDtypeStruct((projection.shape[0] // 2, projection.shape[1]), BF16),
         ],
         scratch_shapes=[
             pltpu.VMEM((rows, width), BF16),
@@ -184,7 +198,7 @@
         ],
         compiler_params=pltpu.CompilerParams(vmem_limit_bytes=32 * 1024 * 1024),
     )(*(pltpu.with_memory_space_constraint(a, pltpu.HBM) for a in args))
-    held = lax.all_to_all(sent.reshape(contexts * SLOTS // 2, 2, BLOCK), "context", 0, 0, tiled=True)
+    held = lax.all_to_all(sent.reshape(contexts * SLOTS // 2, 2, BLOCK), CONTEXT, 0, 0, tiled=True)
     conv = call(
         conv_kernel,
         (contexts * 8, BLOCK),
@@ -197,34 +211,38 @@
         ],
     )
     given = lax.ppermute(leaving, PAIR, [(0, 1), (1, 0)])
-    back = lax.all_to_all(conv.reshape(2 * contexts, 4, BLOCK), ("context", PAIR), 0, 0, tiled=True)
+    places = 2 * Y_FAR
+    around = [(i, (i + 1) % places if i % 2 else (i - 1) % places) for i in range(places)]
+    given_back = lax.ppermute(leaving_back, ("y_far", PAIR), around)
+    back = lax.all_to_all(conv.reshape(2 * contexts, 4, BLOCK), CONTEXT + (PAIR,), 0, 0, tiled=True)
+    gated = call(gate_kernel, (BLOCK, 2 * width), back.reshape(contexts * 8, BLOCK), direct, own_gate, given)
     partial = call(
         project_kernel,
         (tensors, BLOCK, width),
-        back.reshape(contexts * 8, BLOCK),
-        direct,
-        own_gate,
+        gated,
         leaving,
+        leaving_back,
         given,
+        given_back,
     )
     shares = lax.all_to_all(partial, TENSOR, 0, 0, tiled=True)
     return call(sum_kernel, (rows, width), shares)
 
 
 def solution(mesh):
-    contexts = mesh.shape["context"]
-    fine = Mesh(mesh.devices.reshape(contexts, 2, 2, 2), ("context",) + TENSOR)
+    lines = mesh.shape["context"] // Y_FAR
+    fine = Mesh(mesh.devices.reshape(Y_FAR, lines, 2, 2, 2), CONTEXT + TENSOR)
     return jax.shard_map(
         on_device,
         mesh=fine,
         in_specs=(
-            P("context", TENSOR),
-            P("context", TENSOR),
-            P("context", TENSOR),
-            P("context", TENSOR),
+            P(CONTEXT, TENSOR),
+            P(CONTEXT, TENSOR),
+            P(CONTEXT, TENSOR),
+            P(CONTEXT, TENSOR),
             P(TENSOR),
             P(TENSOR, None),
         ),
-        out_specs=P("context", TENSOR),
+        out_specs=P(CONTEXT, TENSOR),
         check_vma=False,
     )

time: 69.6 us -> 68.6 us (0.986)
  waiting for transfers between devices: 9.64 us -> 6 us
  starting transfers between devices: 20.8 us -> 24.4 us
  blocking collectives: 33.2 us -> 32.1 us
    ppermute x0 -> x1, starting transfers between devices: none -> 4.83 us  [on_device(): given_back = lax.ppermute(leaving_back, ('y_far', PAIR), around)]
    all_to_all x1, waiting for transfers between devices: 9.63 us -> 6 us  [on_device(): lax.all_to_all(sent.reshape(contexts * SLOTS // 2, 2, BLOCK), CONTEXT, 0,...]
    all_to_all x1, blocking collectives: 20.1 us -> 18.5 us  [on_device(): lax.all_to_all(conv.reshape(2 * contexts, 4, BLOCK), CONTEXT + (PAIR,), 0...]
    ppermute x1, starting transfers between devices: 3.12 us -> 1.92 us  [on_device(): given = lax.ppermute(leaving, PAIR, [(0, 1), (1, 0)])]
    pallas_call x3 -> x4, Pallas kernels: 3.47 us -> 3.53 us  [call(): pl.pallas_call(kernel, out_shape=jax.ShapeDtypeStruct(shape, BF16), scrat...]
  transfers between devices with their start and end apart: 2 -> 3, of which waited for: 1 -> 1; matrix products, arithmetic and copies ran while one was open for 0% -> 0% of each run, Pallas kernels for 3% -> 3%
where the time goes in v4:
time: 68.6 us; the launch traced here: 68.3 us
  blocking collectives  32.1 us (47%)
  starting transfers between devices  24.4 us (36%)
  waiting for transfers between devices  6 us (9%)
  Pallas kernels  5.78 us (8%)
    all_to_all x1, blocking collectives, on_device(): lax.all_to_all(conv.reshape(2 * contexts, 4, BLOCK), CONTEXT + (PAIR,), 0...  18.5 us
    all_to_all x1, starting transfers between devices, on_device(): lax.all_to_all(sent.reshape(contexts * SLOTS // 2, 2, BLOCK), CONTEXT, 0,...  17.6 us
    all_to_all x1, blocking collectives, on_device(): shares = lax.all_to_all(partial, TENSOR, 0, 0, tiled=True)  13.5 us
    all_to_all x1, waiting for transfers between devices, on_device(): lax.all_to_all(sent.reshape(contexts * SLOTS // 2, 2, BLOCK), CONTEXT, 0,...  6 us
    ppermute x1, starting transfers between devices, on_device(): given_back = lax.ppermute(leaving_back, ('y_far', PAIR), around)  4.83 us
    pallas_call x4, Pallas kernels, call(): pl.pallas_call(kernel, out_shape=jax.ShapeDtypeStruct(shape, BF16), scrat...  3.53 us
    pallas_call x1, Pallas kernels, on_device(): pl.pallas_call(pack_kernel, in_specs=[pl.BlockSpec(memory_space=pltpu.HBM...  2.25 us
    ppermute x1, starting transfers between devices, on_device(): given = lax.ppermute(leaving, PAIR, [(0, 1), (1, 0)])  1.92 us
  transfers between devices with their start and end apart: 3, of which 1 were waited for; matrix products, arithmetic and copies ran while one was open for 0% of the time, Pallas kernels for 3%

profile of v4, /device:TPU:1, one launch (start us, length us, event | category | flops | bytes accessed | tf_op | source)
XLA Modules:
  0.0 68.3 jit_solution(12968635326044199069)
XLA Ops:
  0.0 2.2 %shard_map.64 = (bf16[640,128]{1,0:T(8,128)(2,1)}, f32[128,256]{1,0:T(8,128)S(1)}, bf16[128,256]{1,0:T(8,128)(2,1)S(1)}, bf16[160,2048]{1,0:T(8,128)(2,1)S(1)}, bf16[128,2048]{1,0:T(8,128)(2,1)S(1)}) custom-call(bf16[256,256]{1,0:T(8,128)(2,1)} %refs_0_.1, bf16[256,256]{1,0:T(8,128)(2,1)} %refs_1_.1, f32[16,256]{1,0:T(8,128)} %bitcast.9, f32[1,256]{1,0:T(1,128)} %bitcast.10, ...), custom_call_target="tpu_custom_call" | custom-call | tf_op jit(solution)/shard_map/pallas_call | solution.py:180
  2.3 17.6 %all-to-all-start = ((bf16[320,2,128]{2,1,0:T(2,128)(2,1)}), bf16[320,2,128]{2,1,0:T(2,128)(2,1)S(1)}, u32[]{:S(2)}, u32[]{:S(2)}) async-start(bf16[320,2,128]{2,1,0:T(2,128)(2,1)} %bitcast.2), calls=%async_computation | async-start | bytes 327680 | tf_op jit(solution)/shard_map/all_to_all | solution.py:201
  19.9 4.8 %collective-permute-start.1 = (bf16[128,2048]{1,0:T(8,128)(2,1)S(1)}, bf16[128,2048]{1,0:T(8,128)(2,1)S(1)}, u32[]{:S(2)}, u32[]{:S(2)}) collective-permute-start(bf16[128,2048]{1,0:T(8,128)(2,1)S(1)} %get-tuple-element.14.own_back_ref), channel_id=1, source_target_pairs={{0,385},{1,128},{128,1},{129,256},{256,129},{257,384},{384,257},{3... | collective-permute-start | bytes 1572872 | tf_op jit(solution)/shard_map/ppermute | solution.py:216
  24.7 1.9 %collective-permute-start = (bf16[160,2048]{1,0:T(8,128)(2,1)S(1)}, bf16[160,2048]{1,0:T(8,128)(2,1)S(1)}, u32[]{:S(2)}, u32[]{:S(2)}) collective-permute-start(bf16[160,2048]{1,0:T(8,128)(2,1)S(1)} %get-tuple-element.13.own_ref), channel_id=1, source_target_pairs={{0,1},{1,0},{2,3},{3,2},{4,5},{5,4},{6,7},{7,6},{8,9},{9,8},{10,11... | collective-permute-start | bytes 1966088 | tf_op jit(solution)/shard_map/ppermute | solution.py:213
  26.7 6.0 %all-to-all-done = bf16[320,2,128]{2,1,0:T(2,128)(2,1)S(1)} async-done(((bf16[320,2,128]{2,1,0:T(2,128)(2,1)}), bf16[320,2,128]{2,1,0:T(2,128)(2,1)S(1)}, u32[]{:S(2)}, u32[]{:S(2)}) %all-to-all-start) | async-done | bytes 163872 | tf_op jit(solution)/shard_map/all_to_all | solution.py:201
  32.7 2.0 %shard_map.65 = bf16[512,128]{1,0:T(8,128)(2,1)S(1)} custom-call(bf16[640,128]{1,0:T(8,128)(2,1)S(1)} %bitcast.7), custom_call_target="tpu_custom_call" | custom-call | flops 8000000000 | bytes 300000 | tf_op jit(solution)/shard_map/pallas_call | solution.py:166
  34.7 18.5 %all_to_all.15 = bf16[128,4,128]{2,1,0:T(4,128)(2,1)S(1)} all-to-all(bf16[128,4,128]{2,1,0:T(4,128)(2,1)S(1)} %bitcast.8), channel_id=1, replica_groups=mesh['y_far'=4,'line'=16,'x_far'=2,'x_near'=2,'y_near'=2] {'y_far','line..., dimensions={0} | all-to-all | bytes 262144 | tf_op jit(solution)/shard_map/all_to_all | solution.py:217
  53.2 0.0 collective-permute-done.given_ref
  53.2 0.3 shard_map.66.gated_ref
  53.6 0.0 collective-permute-done.1.given_back_ref
  53.6 0.4 shard_map.67
  54.1 13.5 %all_to_all.16.parts_ref = bf16[8,128,256]{2,1,0:T(8,128)(2,1)S(1)} all-to-all(bf16[8,128,256]{2,1,0:T(8,128)(2,1)S(1)} %shard_map.67), channel_id=1, replica_groups=mesh['y_far'=4,'line'=16,'x_far'=2,'x_near'=2,'y_near'=2] {'x_far','x_ne..., dimensions={0} | all-to-all | bytes 1048576 | tf_op jit(solution)/shard_map/all_to_all | solution.py:228
  67.6 0.7 %shard_map.68 = bf16[256,256]{1,0:T(8,128)(2,1)} custom-call(bf16[8,128,256]{2,1,0:T(8,128)(2,1)S(1)} %all_to_all.16.parts_ref), custom_call_target="tpu_custom_call" | custom-call | tf_op jit(solution)/shard_map/pallas_call | solution.py:166
Async XLA Ops:
  2.3 30.4 %all-to-all-start = ((bf16[320,2,128]{2,1,0:T(2,128)(2,1)}), bf16[320,2,128]{2,1,0:T(2,128)(2,1)S(1)}, u32[]{:S(2)}, u32[]{:S(2)}) async-start(bf16[320,2,128]{2,1,0:T(2,128)(2,1)} %bitcast.2), calls=%async_computation | async-start | bytes 327680 | tf_op jit(solution)/shard_map/all_to_all | solution.py:201
  19.9 33.7 %collective-permute-start.1 = (bf16[128,2048]{1,0:T(8,128)(2,1)S(1)}, bf16[128,2048]{1,0:T(8,128)(2,1)S(1)}, u32[]{:S(2)}, u32[]{:S(2)}) collective-permute-start(bf16[128,2048]{1,0:T(8,128)(2,1)S(1)} %get-tuple-element.14.own_back_ref), channel_id=1, source_target_pairs={{0,385},{1,128},{128,1},{129,256},{256,129},{257,384},{384,257},{3... | collective-permute-start | bytes 1572872 | tf_op jit(solution)/shard_map/ppermute | solution.py:216
  24.7 28.5 %collective-permute-start = (bf16[160,2048]{1,0:T(8,128)(2,1)S(1)}, bf16[160,2048]{1,0:T(8,128)(2,1)S(1)}, u32[]{:S(2)}, u32[]{:S(2)}) collective-permute-start(bf16[160,2048]{1,0:T(8,128)(2,1)S(1)} %get-tuple-element.13.own_ref), channel_id=1, source_target_pairs={{0,1},{1,0},{2,3},{3,2},{4,5},{5,4},{6,7},{7,6},{8,9},{9,8},{10,11... | collective-permute-start | bytes 1966088 | tf_op jit(solution)/shard_map/ppermute | solution.py:213

commit v5 on v4

--- a/solution.py
+++ b/solution.py
@@ -11,7 +11,7 @@
 CONTEXT = ("y_far", "line")
 TENSOR = ("x_far", "x_near", "y_near")
 PAIR = "y_near"
-PIECES = 8
+PIECES = 2
 SHARE = 16
 F32 = jnp.float32
 BF16 = jnp.bfloat16
@@ -92,7 +92,6 @@
     for m in range(4):
         moved = x if m == 0 else jnp.concatenate([jnp.zeros((4 * m, BLOCK), F32), x[: rows - 4 * m]], axis=0)
         lhs_ref[:, m * BLOCK : (m + 1) * BLOCK] = moved.astype(BF16)
-    acc_ref[...] = jnp.zeros_like(acc_ref)
     keep = iota((BLOCK, BLOCK), 1) >= iota((BLOCK, BLOCK), 0)
 
     def turned(block):
@@ -115,7 +114,11 @@
                     last[side] = now
                 sides.append(jnp.concatenate(stack, axis=0))
             both = jnp.concatenate(sides, axis=1)
-            acc_ref[4 * q :, :] += jnp.dot(lhs_ref[: rows - 4 * q, :], both, preferred_element_type=F32)
+            part = jnp.dot(lhs_ref[: rows - 4 * q, :], both, preferred_element_type=F32)
+            if q == 0:
+                acc_ref[...] = part
+            else:
+                acc_ref[4 * q :, :] += part
     moved = 4 * step
     out_ref[:moved, :] = acc_ref[:moved, :BLOCK].astype(BF16)
     out_ref[moved:, :] = (acc_ref[moved:, :BLOCK] + acc_ref[: rows - moved, BLOCK:]).astype(BF16)
@@ -151,15 +154,21 @@
         out_ref[k] = total.astype(BF16)
 
 
-def sum_kernel(parts_ref, out_ref):
+def sum_kernel(parts_ref, out_hbm, total_ref, sems):
     step = {"x_far": 4, "x_near": 2, "y_near": 1}[PAIR]
+    moves = []
     for side in range(2):
         total = None
         for k in range(parts_ref.shape[0]):
             if k // step % 2 == side:
                 part = parts_ref[k].astype(F32)
                 total = part if total is None else total + part
-        out_ref[side * BLOCK : (side + 1) * BLOCK, :] = total.astype(BF16)
+        half = pl.ds(side * BLOCK, BLOCK)
+        total_ref[half, :] = total.astype(BF16)
+        moves.append(pltpu.make_async_copy(total_ref.at[half], out_hbm.at[half], sems.at[side]))
+        moves[-1].start()
+    for move in moves:
+        move.wait()
 
 
 def call(kernel, shape, *args, scratch=(), cost=None):
@@ -226,7 +235,13 @@
         given_back,
     )
     shares = lax.all_to_all(partial, TENSOR, 0, 0, tiled=True)
-    return call(sum_kernel, (rows, width), shares)
+    return pl.pallas_call(
+        sum_kernel,
+        out_shape=pltpu.HBM((rows, width), BF16),
+        out_specs=pl.BlockSpec(memory_space=pltpu.HBM),
+        scratch_shapes=[pltpu.VMEM((rows, width), BF16), pltpu.SemaphoreType.DMA((2,))],
+        compiler_params=pltpu.CompilerParams(vmem_limit_bytes=32 * 1024 * 1024),
+    )(shares)
 
 
 def solution(mesh):

time: 68.6 us -> 68.6 us (level)
    pallas_call x4 -> x3, Pallas kernels: 3.53 us -> 2.81 us  [call(): pl.pallas_call(kernel, out_shape=jax.ShapeDtypeStruct(shape, BF16), scrat...]
    pallas_call x0 -> x1, Pallas kernels: none -> 0.71 us  [on_device(): pl.pallas_call(sum_kernel, out_shape=pltpu.HBM((rows, width), BF16), out_...]
where the time goes in v5:
time: 68.6 us; the launch traced here: 68.3 us
  blocking collectives  32.1 us (47%)
  starting transfers between devices  24.4 us (36%)
  waiting for transfers between devices  6 us (9%)
  Pallas kernels  5.71 us (8%)
    all_to_all x1, blocking collectives, on_device(): lax.all_to_all(conv.reshape(2 * contexts, 4, BLOCK), CONTEXT + (PAIR,), 0...  18.5 us
    all_to_all x1, starting transfers between devices, on_device(): lax.all_to_all(sent.reshape(contexts * SLOTS // 2, 2, BLOCK), CONTEXT, 0,...  17.6 us
    all_to_all x1, blocking collectives, on_device(): shares = lax.all_to_all(partial, TENSOR, 0, 0, tiled=True)  13.5 us
    all_to_all x1, waiting for transfers between devices, on_device(): lax.all_to_all(sent.reshape(contexts * SLOTS // 2, 2, BLOCK), CONTEXT, 0,...  6 us
    ppermute x1, starting transfers between devices, on_device(): given_back = lax.ppermute(leaving_back, ('y_far', PAIR), around)  4.83 us
    pallas_call x3, Pallas kernels, call(): pl.pallas_call(kernel, out_shape=jax.ShapeDtypeStruct(shape, BF16), scrat...  2.81 us
    pallas_call x1, Pallas kernels, on_device(): pl.pallas_call(pack_kernel, in_specs=[pl.BlockSpec(memory_space=pltpu.HBM...  2.19 us
    ppermute x1, starting transfers between devices, on_device(): given = lax.ppermute(leaving, PAIR, [(0, 1), (1, 0)])  1.92 us
  transfers between devices with their start and end apart: 3, of which 1 were waited for; matrix products, arithmetic and copies ran while one was open for 0% of the time, Pallas kernels for 3%

profile of v5, /device:TPU:1, one launch (start us, length us, event | category | flops | bytes accessed | tf_op | source)
XLA Modules:
  0.0 68.3 jit_solution(3253967180683843520)
XLA Ops:
  0.0 2.2 %shard_map.64 = (bf16[640,128]{1,0:T(8,128)(2,1)}, f32[128,256]{1,0:T(8,128)S(1)}, bf16[128,256]{1,0:T(8,128)(2,1)S(1)}, bf16[160,2048]{1,0:T(8,128)(2,1)S(1)}, bf16[128,2048]{1,0:T(8,128)(2,1)S(1)}) custom-call(bf16[256,256]{1,0:T(8,128)(2,1)} %refs_0_.1, bf16[256,256]{1,0:T(8,128)(2,1)} %refs_1_.1, f32[16,256]{1,0:T(8,128)} %bitcast.9, f32[1,256]{1,0:T(1,128)} %bitcast.10, ...), custom_call_target="tpu_custom_call" | custom-call | tf_op jit(solution)/shard_map/pallas_call | solution.py:189
  2.2 17.6 %all-to-all-start = ((bf16[320,2,128]{2,1,0:T(2,128)(2,1)}), bf16[320,2,128]{2,1,0:T(2,128)(2,1)S(1)}, u32[]{:S(2)}, u32[]{:S(2)}) async-start(bf16[320,2,128]{2,1,0:T(2,128)(2,1)} %bitcast.2), calls=%async_computation | async-start | bytes 327680 | tf_op jit(solution)/shard_map/all_to_all | solution.py:210
  19.9 4.8 %collective-permute-start.1 = (bf16[128,2048]{1,0:T(8,128)(2,1)S(1)}, bf16[128,2048]{1,0:T(8,128)(2,1)S(1)}, u32[]{:S(2)}, u32[]{:S(2)}) collective-permute-start(bf16[128,2048]{1,0:T(8,128)(2,1)S(1)} %get-tuple-element.14.own_back_ref), channel_id=1, source_target_pairs={{0,385},{1,128},{128,1},{129,256},{256,129},{257,384},{384,257},{3... | collective-permute-start | bytes 1572872 | tf_op jit(solution)/shard_map/ppermute | solution.py:225
  24.7 1.9 %collective-permute-start = (bf16[160,2048]{1,0:T(8,128)(2,1)S(1)}, bf16[160,2048]{1,0:T(8,128)(2,1)S(1)}, u32[]{:S(2)}, u32[]{:S(2)}) collective-permute-start(bf16[160,2048]{1,0:T(8,128)(2,1)S(1)} %get-tuple-element.13.own_ref), channel_id=1, source_target_pairs={{0,1},{1,0},{2,3},{3,2},{4,5},{5,4},{6,7},{7,6},{8,9},{9,8},{10,11... | collective-permute-start | bytes 1966088 | tf_op jit(solution)/shard_map/ppermute | solution.py:222
  26.6 6.0 %all-to-all-done = bf16[320,2,128]{2,1,0:T(2,128)(2,1)S(1)} async-done(((bf16[320,2,128]{2,1,0:T(2,128)(2,1)}), bf16[320,2,128]{2,1,0:T(2,128)(2,1)S(1)}, u32[]{:S(2)}, u32[]{:S(2)}) %all-to-all-start) | async-done | bytes 163872 | tf_op jit(solution)/shard_map/all_to_all | solution.py:210
  32.6 2.0 %shard_map.65 = bf16[512,128]{1,0:T(8,128)(2,1)S(1)} custom-call(bf16[640,128]{1,0:T(8,128)(2,1)S(1)} %bitcast.7), custom_call_target="tpu_custom_call" | custom-call | flops 8000000000 | bytes 300000 | tf_op jit(solution)/shard_map/pallas_call | solution.py:175
  34.6 18.5 %all_to_all.15 = bf16[128,4,128]{2,1,0:T(4,128)(2,1)S(1)} all-to-all(bf16[128,4,128]{2,1,0:T(4,128)(2,1)S(1)} %bitcast.8), channel_id=1, replica_groups=mesh['y_far'=4,'line'=16,'x_far'=2,'x_near'=2,'y_near'=2] {'y_far','line..., dimensions={0} | all-to-all | bytes 262144 | tf_op jit(solution)/shard_map/all_to_all | solution.py:226
  53.2 0.0 collective-permute-done.given_ref
  53.2 0.4 shard_map.66.gated_ref
  53.5 0.0 collective-permute-done.1.given_back_ref
  53.5 0.4 shard_map.67
  54.0 13.5 %all_to_all.16.parts_ref = bf16[8,128,256]{2,1,0:T(8,128)(2,1)S(1)} all-to-all(bf16[8,128,256]{2,1,0:T(8,128)(2,1)S(1)} %shard_map.67), channel_id=1, replica_groups=mesh['y_far'=4,'line'=16,'x_far'=2,'x_near'=2,'y_near'=2] {'x_far','x_ne..., dimensions={0} | all-to-all | bytes 1048576 | tf_op jit(solution)/shard_map/all_to_all | solution.py:237
  67.5 0.7 %shard_map.68 = bf16[256,256]{1,0:T(8,128)(2,1)} custom-call(bf16[8,128,256]{2,1,0:T(8,128)(2,1)S(1)} %all_to_all.16.parts_ref), custom_call_target="tpu_custom_call" | custom-call | tf_op jit(solution)/shard_map/pallas_call | solution.py:238
Async XLA Ops:
  2.2 30.4 %all-to-all-start = ((bf16[320,2,128]{2,1,0:T(2,128)(2,1)}), bf16[320,2,128]{2,1,0:T(2,128)(2,1)S(1)}, u32[]{:S(2)}, u32[]{:S(2)}) async-start(bf16[320,2,128]{2,1,0:T(2,128)(2,1)} %bitcast.2), calls=%async_computation | async-start | bytes 327680 | tf_op jit(solution)/shard_map/all_to_all | solution.py:210
  19.9 33.7 %collective-permute-start.1 = (bf16[128,2048]{1,0:T(8,128)(2,1)S(1)}, bf16[128,2048]{1,0:T(8,128)(2,1)S(1)}, u32[]{:S(2)}, u32[]{:S(2)}) collective-permute-start(bf16[128,2048]{1,0:T(8,128)(2,1)S(1)} %get-tuple-element.14.own_back_ref), channel_id=1, source_target_pairs={{0,385},{1,128},{128,1},{129,256},{256,129},{257,384},{384,257},{3... | collective-permute-start | bytes 1572872 | tf_op jit(solution)/shard_map/ppermute | solution.py:225
  24.7 28.5 %collective-permute-start = (bf16[160,2048]{1,0:T(8,128)(2,1)S(1)}, bf16[160,2048]{1,0:T(8,128)(2,1)S(1)}, u32[]{:S(2)}, u32[]{:S(2)}) collective-permute-start(bf16[160,2048]{1,0:T(8,128)(2,1)S(1)} %get-tuple-element.13.own_ref), channel_id=1, source_target_pairs={{0,1},{1,0},{2,3},{3,2},{4,5},{5,4},{6,7},{7,6},{8,9},{9,8},{10,11... | collective-permute-start | bytes 1966088 | tf_op jit(solution)/shard_map/ppermute | solution.py:222
